TPU v7x, 32 devices: a whole 2x2x4 slice. The times are simulated.
32 devices in a mesh: dp: 2 (over core), pipe: 2 (over x), ctx: 8 (over z, y).
Axes of the slice: x: 2, y: 2, z: 4, core: 2. Of those that a mesh axis runs over, the one named last changes fastest.
Arguments:
- queries: bfloat16 [4, 1024, 2048], P(('dp', 'pipe'), 'ctx'), parts along dimension 0, may hold values from -6 to 6
- section_key_state: bfloat16 [4, 1024, 256], P(('dp', 'pipe'), 'ctx'), parts along dimension 0, may hold values from -6 to 6
- section_value_state: bfloat16 [4, 1024, 256], P(('dp', 'pipe'), 'ctx'), parts along dimension 0, may hold values from -6 to 6
- out_grad: bfloat16 [4, 1024, 2048], P(('dp', 'pipe'), 'ctx'), parts along dimension 0, may hold values from -6 to 6
- doc_blocks: int32 [4, 4], P(('dp', 'pipe')), parts along dimension 0, may hold values from 1 to 4, 8 in all within a row
Outputs:
- attention: bfloat16 [4, 1024, 2048], P(('dp', 'pipe'), 'ctx'), parts along dimension 0
- query_grads: bfloat16 [4, 1024, 2048], P(('dp', 'pipe'), 'ctx'), parts along dimension 0
- key_grads: bfloat16 [4, 1024, 256], P(('dp', 'pipe'), 'ctx'), parts along dimension 0
- value_grads: bfloat16 [4, 1024, 256], P(('dp', 'pipe'), 'ctx'), parts along dimension 0
There are 2 independent parts, one for each index of `dp`. A program takes and returns all parts, laid end to end along the dimension named above; each array names one. Nothing has to cross between parts.
Inputs may be any that keep to these rules, and one draw needn't show every extreme that they name: `doc_blocks`: each row sums to 8, and one document of each row has exactly 4 blocks.
All inputs are finite; a program needn't handle non-finite values.
Results may differ from a plain program's by a relative error of at most 0.012.
The roundings to bfloat16 on the way count: a program that leaves them out, or rounds other values in their place, can miss the bound.
Values may be sent and summed in bfloat16 or wider, within the bound.
A program may use at most 64 MiB of HBM per device.

v0:
```python
import math
import jax
import jax.numpy as jnp
from jax import lax
from jax.sharding import PartitionSpec as P

QUERY_HEAD_COUNT = 16
KEY_VALUE_HEADS = 2
HEAD_SIZE = 128
BLK = 128


def from_behind(x, axis, by):
    length = lax.axis_size(axis)
    pairs = [(i, i + by) for i in range(length) if 0 <= i + by < length]
    return lax.ppermute(x, axis, pairs)


def layout_positions(device_at, shard_rows, shard_count):
    half_rows = shard_rows // 2
    offsets = jnp.arange(half_rows, dtype=jnp.int32)
    lower_half = device_at * half_rows + offsets
    upper_half = (2 * shard_count - 1 - device_at) * half_rows + offsets
    return jnp.concatenate([lower_half, upper_half], axis=-1).reshape(-1)


def document_of(positions, doc_lengths):
    bounds = (jnp.cumsum(doc_lengths) * BLK)[:-1]
    return jnp.sum((positions[:, None] >= bounds[None, :]).astype(jnp.int32), axis=1)


def to_groups(score_matrix, shard_rows, group_width):
    grouped_heads = score_matrix.reshape(
        shard_rows, KEY_VALUE_HEADS, group_width, HEAD_SIZE
    ).transpose(1, 2, 0, 3)
    return grouped_heads.reshape(KEY_VALUE_HEADS, group_width * shard_rows, HEAD_SIZE)


def from_groups(stacked_values, shard_rows, group_width):
    spread_rows = stacked_values.reshape(
        KEY_VALUE_HEADS, group_width, shard_rows, HEAD_SIZE
    ).transpose(2, 0, 1, 3)
    return spread_rows.reshape(shard_rows, QUERY_HEAD_COUNT * HEAD_SIZE)


def local(queries, section_key_state, section_value_state, out_grad, doc_blocks):
    shard_count = lax.axis_size("ctx")
    shard_rows = queries.shape[1]
    sequence = shard_rows * shard_count
    group_width = QUERY_HEAD_COUNT // KEY_VALUE_HEADS
    piled_rows = group_width * shard_rows
    inverse_root = 1.0 / math.sqrt(HEAD_SIZE)
    block_size = min(512, sequence)
    block_count = sequence // block_size
    term_columns = 2 * KEY_VALUE_HEADS * HEAD_SIZE
    doc_lengths = doc_blocks[0]
    query_pos = layout_positions(lax.axis_index("ctx"), shard_rows, shard_count)
    key_pos = layout_positions(
        jnp.arange(shard_count, dtype=jnp.int32)[:, None], shard_rows, shard_count
    )
    query_doc = document_of(query_pos, doc_lengths)
    key_doc = document_of(key_pos, doc_lengths)
    query_groups = to_groups(queries[0], shard_rows, group_width)
    grad_groups = to_groups(out_grad[0], shard_rows, group_width)
    key_all, value_all = (
        lax.all_gather(section_key_state[0], "ctx", axis=0, tiled=True),
        lax.all_gather(section_value_state[0], "ctx", axis=0, tiled=True),
    )

    def block_inputs(first_row, total_size):
        block_pos = lax.dynamic_slice_in_dim(key_pos, first_row, total_size)
        block_doc = lax.dynamic_slice_in_dim(key_doc, first_row, total_size)
        visible = (query_doc[:, None] == block_doc[None, :]) & (
            block_pos[None, :] <= query_pos[:, None]
        )
        visible = jnp.tile(visible, (group_width, 1))[None]
        key_block = (
            lax.dynamic_slice_in_dim(key_all, first_row, total_size)
            .reshape(total_size, KEY_VALUE_HEADS, HEAD_SIZE)
            .transpose(1, 0, 2)
        )
        value_block = (
            lax.dynamic_slice_in_dim(value_all, first_row, total_size)
            .reshape(total_size, KEY_VALUE_HEADS, HEAD_SIZE)
            .transpose(1, 0, 2)
        )
        return (visible, key_block, value_block)

    def scores_of(visible, key_block):
        scores = jnp.einsum(
            "gqd,gsd->gqs", query_groups, key_block, preferred_element_type=jnp.float32
        )
        return jnp.where(visible, scores * inverse_root, -jnp.inf)

    def stat_step(block_at, carried):
        running_max, running_sum = carried
        visible, key_block, value_block = block_inputs(block_at * block_size, block_size)
        scores = scores_of(visible, key_block)
        new_max = jnp.maximum(running_max, jnp.max(scores, axis=-1))
        new_sum = running_sum * jnp.exp(running_max - new_max)
        new_sum = new_sum + jnp.sum(jnp.exp(scores - new_max[..., None]), axis=-1)
        return (new_max, new_sum)

    initial_max = jnp.full((KEY_VALUE_HEADS, piled_rows), -1e30, jnp.float32)
    initial_sum = jnp.zeros((KEY_VALUE_HEADS, piled_rows), jnp.float32)
    final_max, final_sum = lax.fori_loop(0, block_count, stat_step, (initial_max, initial_sum))
    log_total = final_max + jnp.log(final_sum)

    def out_step(block_at, accumulated):
        visible, key_block, value_block = block_inputs(block_at * block_size, block_size)
        weights_low = jnp.exp(scores_of(visible, key_block) - log_total[..., None]).astype(
            jnp.bfloat16
        )
        return accumulated + jnp.einsum(
            "gqs,gsd->gqd", weights_low, value_block, preferred_element_type=jnp.float32
        )

    blank_output = jnp.zeros((KEY_VALUE_HEADS, piled_rows, HEAD_SIZE), jnp.float32)
    out_groups = lax.fori_loop(0, block_count, out_step, blank_output).astype(jnp.bfloat16)
    row_dot = jnp.sum(grad_groups.astype(jnp.float32) * out_groups.astype(jnp.float32), axis=-1)

    def grads_of(visible, key_block, value_block):
        weights = jnp.exp(scores_of(visible, key_block) - log_total[..., None])
        weight_grad = jnp.einsum(
            "gqd,gsd->gqs", grad_groups, value_block, preferred_element_type=jnp.float32
        )
        score_grad = (weights * (weight_grad - row_dot[..., None]) * inverse_root).astype(
            jnp.bfloat16
        )
        return (weights.astype(jnp.bfloat16), score_grad)

    def key_terms(weights_low, score_grad, total_size):
        key_term = jnp.einsum(
            "gqs,gqd->sgd", score_grad, query_groups, preferred_element_type=jnp.float32
        ).reshape(total_size, KEY_VALUE_HEADS * HEAD_SIZE)
        value_term = jnp.einsum(
            "gqs,gqd->sgd", weights_low, grad_groups, preferred_element_type=jnp.float32
        ).reshape(total_size, KEY_VALUE_HEADS * HEAD_SIZE)
        return jnp.concatenate([key_term, value_term], axis=-1)

    def back_step(query_grad, block_at):
        visible, key_block, value_block = block_inputs(block_at * block_size, block_size)
        weights_low, score_grad = grads_of(visible, key_block, value_block)
        new_grad = query_grad + jnp.einsum(
            "gqs,gsd->gqd", score_grad, key_block, preferred_element_type=jnp.float32
        )
        return (new_grad, key_terms(weights_low, score_grad, block_size))

    blank_gradient = jnp.zeros((KEY_VALUE_HEADS, piled_rows, HEAD_SIZE), jnp.float32)
    query_grad, block_terms = lax.scan(
        back_step, blank_gradient, jnp.arange(block_count, dtype=jnp.int32)
    )
    query_rows = from_groups(query_grad.astype(jnp.bfloat16), shard_rows, group_width)
    pair_sum = lax.psum_scatter(
        block_terms.reshape(sequence, term_columns).astype(jnp.bfloat16),
        "ctx",
        scatter_dimension=0,
        tiled=True,
    )
    joined = jnp.concatenate([query_rows, pair_sum], axis=-1)[None]
    sent_back = from_behind(joined, "pipe", -1)
    query_sent = sent_back[:, :, : QUERY_HEAD_COUNT * HEAD_SIZE]
    pair_passed = sent_back[:, :, QUERY_HEAD_COUNT * HEAD_SIZE :]
    attention = from_groups(out_groups, shard_rows, group_width)[None]
    key_passed = pair_passed[:, :, : KEY_VALUE_HEADS * HEAD_SIZE]
    value_passed = pair_passed[:, :, KEY_VALUE_HEADS * HEAD_SIZE :]
    return (attention, query_sent, key_passed, value_passed)


def solution(mesh):
    return jax.shard_map(
        local,
        mesh=mesh,
        in_specs=(
            P(("dp", "pipe"), "ctx", None),
            P(("dp", "pipe"), "ctx", None),
            P(("dp", "pipe"), "ctx", None),
            P(("dp", "pipe"), "ctx", None),
            P(("dp", "pipe"), None),
        ),
        out_specs=(
            P(("dp", "pipe"), "ctx", None),
            P(("dp", "pipe"), "ctx", None),
            P(("dp", "pipe"), "ctx", None),
            P(("dp", "pipe"), "ctx", None),
        ),
        check_vma=False,
    )
```

profile of v0, /device:TPU:0, one launch (start us, length us, event | category | flops | bytes accessed | tf_op | source)
XLA Modules:
  0.0 227.1 jit_solution(4679452469479922389)
XLA Ops:
  7.3 0.8 reduce-window.9
  8.5 1.1 copy.93
  9.7 0.6 copy.75
  10.9 29.5 %all-gather = bf16[1,1024,256]{1,2,0:T(8,128)(2,1)S(1)} all-gather(bf16[1,128,256]{1,2,0:T(8,128)(2,1)S(1)} %copy.74), channel_id=2, replica_groups=mesh['dp'=2,'pipe'=2,'ctx'=8] {'ctx'}, dimensions={1}, use_global_device_ids=true | all-gather | bytes 589824 | tf_op jit(solution)/shard_map/all_gather | solution.py:66
  40.5 14.3 %while.43 = (s32[]{:T(128)}, f32[2,1024]{1,0:T(2,128)S(1)}, f32[2,1024]{1,0:T(2,128)S(1)}, s32[128]{0:T(128)S(1)}, s32[1024]{0:T(1024)S(1)}, /*index=5*/s32[1024...) while((s32[]{:T(128)}, f32[2,1024]{1,0:T(2,128)S(1)}, ...), condition=%wide.region_6.7_spmd.clone, body=%wide.region_3.6_spmd.clone.sunk | while | flops 275982336 | bytes 13096130 | solution.py:106
  41.6 2.8 %fusion.64 = (f32[2,1024]{1,0:T(2,128)S(1)}, f32[2,512,1024]{2,1,0:T(8,128)}) fusion(pred[1024,512]{0,1:T(8,128)(4,1)S(1)} %bitcast.211, bf16[2,1024,128]{2,1,0:T(8,128)(2,1)S(1)} %get-tuple-element.915, bf16[512,2,128]{2,0,1:T(8,128)(2,1)S(1)} %copy.114), kind=kOutput, calls=%fused_computation.2.clone.1 | convolution fusion | flops 271579136 | bytes 5513216 | tf_op jit(solution)/shard_map/while/body/eval_jaxpr/gqd,gsd->gqs/dot_general | solution.py:90
  44.4 3.2 %exponential_reduce_fusion.2 = f32[2,1024]{1,0:T(2,128)S(1)} fusion(f32[2,512,1024]{2,1,0:T(8,128)} %get-tuple-element.852, f32[2,1024]{1,0:T(2,128)S(1)} %fusion.65, pred[1024,512]{0,1:T(8,128)(4,1)S(1)} %bitcast.212), kind=kLoop, calls=%fused_computation.1.clone.1 | loop fusion | flops 4192256 | bytes 4734976 | tf_op jit(solution)/shard_map/while/body/eval_jaxpr/reduce_sum | solution.py:101
  48.7 2.8 %fusion.64 = (f32[2,1024]{1,0:T(2,128)S(1)}, f32[2,512,1024]{2,1,0:T(8,128)}) fusion(pred[1024,512]{0,1:T(8,128)(4,1)S(1)} %bitcast.211, bf16[2,1024,128]{2,1,0:T(8,128)(2,1)S(1)} %get-tuple-element.915, bf16[512,2,128]{2,0,1:T(8,128)(2,1)S(1)} %copy.114), kind=kOutput, calls=%fused_computation.2.clone.1 | convolution fusion | flops 271579136 | bytes 5513216 | tf_op jit(solution)/shard_map/while/body/eval_jaxpr/gqd,gsd->gqs/dot_general | solution.py:90
  51.6 3.2 %exponential_reduce_fusion.2 = f32[2,1024]{1,0:T(2,128)S(1)} fusion(f32[2,512,1024]{2,1,0:T(8,128)} %get-tuple-element.852, f32[2,1024]{1,0:T(2,128)S(1)} %fusion.65, pred[1024,512]{0,1:T(8,128)(4,1)S(1)} %bitcast.212), kind=kLoop, calls=%fused_computation.1.clone.1 | loop fusion | flops 4192256 | bytes 4734976 | tf_op jit(solution)/shard_map/while/body/eval_jaxpr/reduce_sum | solution.py:101
  54.9 28.8 %all-gather.1 = bf16[1,1024,256]{1,2,0:T(8,128)(2,1)} all-gather(bf16[1,128,256]{1,2,0:T(8,128)(2,1)S(1)} %copy.77), channel_id=3, replica_groups=mesh['dp'=2,'pipe'=2,'ctx'=8] {'ctx'}, dimensions={1}, use_global_device_ids=true | all-gather | bytes 589824 | tf_op jit(solution)/shard_map/all_gather | solution.py:67
  83.8 11.5 %while.44 = (s32[]{:T(128)}, f32[2,1024,128]{2,1,0:T(8,128)}, s32[128]{0:T(128)S(1)}, s32[1024]{0:T(1024)S(1)}, s32[1024]{0:T(1024)S(1)}, /*index=5*/s32[128]{0:...) while((s32[]{:T(128)}, f32[2,1024,128]{2,1,0:T(8,128)}, ...), condition=%wide.region_8.9_spmd.clone, body=%wide.region_7.8_spmd.clone.sunk | while | flops 541786112 | bytes 7492809 | solution.py:119
  84.6 1.0 constant_dynamic-slice_fusion.9
  86.0 2.9 %fusion.70 = f32[2,1024,128]{2,1,0:T(8,128)} fusion(bf16[2,1024,128]{2,1,0:T(8,128)(2,1)S(1)} %get-tuple-element.955, f32[2,1024]{1,0:T(2,128)S(1)} %get-tuple-element.956, pred[1024,512]{0,1:T(8,128)(4,1)S(1)} %bitcast.225, f32[2,1024,128]{2,1,0:T(8,128)} %get-tuple-element.935, pred[]{:T(512)S(6)} %compare.10, ...), kind=kOutput, calls=%fused_computation.18.clone.1 | convolution fusion | flops 541589504 | bytes 3678209 | tf_op jit(solution)/shard_map/while/body/eval_jaxpr/gqs,gsd->gqd/dot_general | solution.py:114
  89.8 1.0 constant_dynamic-slice_fusion.9
  91.1 4.1 %fusion.70 = f32[2,1024,128]{2,1,0:T(8,128)} fusion(bf16[2,1024,128]{2,1,0:T(8,128)(2,1)S(1)} %get-tuple-element.955, f32[2,1024]{1,0:T(2,128)S(1)} %get-tuple-element.956, pred[1024,512]{0,1:T(8,128)(4,1)S(1)} %bitcast.225, f32[2,1024,128]{2,1,0:T(8,128)} %get-tuple-element.935, pred[]{:T(512)S(6)} %compare.10, ...), kind=kOutput, calls=%fused_computation.18.clone.1 | convolution fusion | flops 541589504 | bytes 3678209 | tf_op jit(solution)/shard_map/while/body/eval_jaxpr/gqs,gsd->gqd/dot_general | solution.py:114
  95.2 1.4 copy.79
  96.8 0.6 copy.81
  97.4 1.0 reshape.296
  98.4 1.2 multiply_reduce_fusion
  99.7 37.0 %while.45 = (s32[]{:T(128)}, f32[2,1024,128]{2,1,0:T(8,128)}, bf16[2,512,512]{1,2,0:T(8,128)(2,1)}, s32[128]{0:T(128)S(1)}, s32[2]{0:T(128)S(1)}, /*index=5*/s32...) while((s32[]{:T(128)}, f32[2,1024,128]{2,1,0:T(8,128)}, ...), condition=%wide.region_11.12_spmd.clone, body=%wide.region_10.11_spmd.clone.sunk | while | flops 1355481088 | bytes 49190700 | solution.py:150
  99.7 0.6 dynamic_slice.99
  101.6 1.1 copy.119
  102.6 1.0 constant_dynamic-slice_fusion.10
  103.8 2.6 %fusion.81 = f32[2,512,1024]{2,1,0:T(8,128)} fusion(bf16[2,1024,128]{1,2,0:T(8,128)(2,1)S(1)} %get-tuple-element.1007, bf16[512,2,128]{2,0,1:T(8,128)(2,1)S(1)} %copy.118), kind=kOutput, calls=%fused_computation.41.clone.1 | convolution fusion | flops 268435456 | bytes 4980736 | tf_op jit(solution)/shard_map/while/body/eval_jaxpr/gqd,gsd->gqs/dot_general | solution.py:90
  106.4 0.9 copy.120
  107.3 4.3 %fusion.82 = bf16[2,1024,512]{1,2,0:T(8,128)(2,1)S(1)} fusion(f32[2,512,1024]{2,1,0:T(8,128)} %fusion.81, bf16[2,1024,128]{1,2,0:T(8,128)(2,1)} %get-tuple-element.1010, f32[2,1024]{1,0:T(2,128)S(1)} %get-tuple-element.1011, f32[2,1024]{1,0:T(2,128)S(1)} %get-tuple-element.1008, pred[1024,512]{0,1:T(8,128)(4,1)} %bitcast.223, ...), kind=kOutput, calls=%fused_computation.28.clone.1 | convolution fusion | flops 275775488 | bytes 7618560 | tf_op jit(solution)/shard_map/while/body/eval_jaxpr/gqd,gsd->gqs/dot_general | solution.py:124
  111.6 0.8 fusion.84
  112.5 2.4 %fusion.83 = bf16[2,512,128]{1,2,0:T(8,128)(2,1)S(1)} fusion(bf16[2,1024,128]{1,2,0:T(8,128)(2,1)} %get-tuple-element.1010, f32[2,512,1024]{2,1,0:T(8,128)S(1)} %copy-done, f32[2,1024]{1,0:T(2,128)S(1)} %get-tuple-element.1008, pred[1024,512]{0,1:T(8,128)(4,1)S(1)} %bitcast.224), kind=kOutput, calls=%fused_computation.33.clone.1 | convolution fusion | flops 272629760 | bytes 5513216 | tf_op jit(solution)/shard_map/while/body/eval_jaxpr/gqs,gqd->sgd/dot_general | solution.py:136
  114.8 0.8 fusion.85
  115.7 1.9 convolution_add_fusion.2
  119.4 1.1 copy.119
  120.5 1.0 constant_dynamic-slice_fusion.10
  121.7 2.6 %fusion.81 = f32[2,512,1024]{2,1,0:T(8,128)} fusion(bf16[2,1024,128]{1,2,0:T(8,128)(2,1)S(1)} %get-tuple-element.1007, bf16[512,2,128]{2,0,1:T(8,128)(2,1)S(1)} %copy.118), kind=kOutput, calls=%fused_computation.41.clone.1 | convolution fusion | flops 268435456 | bytes 4980736 | tf_op jit(solution)/shard_map/while/body/eval_jaxpr/gqd,gsd->gqs/dot_general | solution.py:90
  124.3 0.9 copy.120
  125.2 4.3 %fusion.82 = bf16[2,1024,512]{1,2,0:T(8,128)(2,1)S(1)} fusion(f32[2,512,1024]{2,1,0:T(8,128)} %fusion.81, bf16[2,1024,128]{1,2,0:T(8,128)(2,1)} %get-tuple-element.1010, f32[2,1024]{1,0:T(2,128)S(1)} %get-tuple-element.1011, f32[2,1024]{1,0:T(2,128)S(1)} %get-tuple-element.1008, pred[1024,512]{0,1:T(8,128)(4,1)} %bitcast.223, ...), kind=kOutput, calls=%fused_computation.28.clone.1 | convolution fusion | flops 275775488 | bytes 7618560 | tf_op jit(solution)/shard_map/while/body/eval_jaxpr/gqd,gsd->gqs/dot_general | solution.py:124
  129.5 0.8 fusion.84
  130.3 2.4 %fusion.83 = bf16[2,512,128]{1,2,0:T(8,128)(2,1)S(1)} fusion(bf16[2,1024,128]{1,2,0:T(8,128)(2,1)} %get-tuple-element.1010, f32[2,512,1024]{2,1,0:T(8,128)S(1)} %copy-done, f32[2,1024]{1,0:T(2,128)S(1)} %get-tuple-element.1008, pred[1024,512]{0,1:T(8,128)(4,1)S(1)} %bitcast.224), kind=kOutput, calls=%fused_computation.33.clone.1 | convolution fusion | flops 272629760 | bytes 5513216 | tf_op jit(solution)/shard_map/while/body/eval_jaxpr/gqs,gqd->sgd/dot_general | solution.py:136
  132.7 0.8 fusion.85
  133.5 3.1 %convolution_add_fusion.2 = f32[2,1024,128]{2,1,0:T(8,128)} fusion(bf16[2,1024,512]{1,2,0:T(8,128)(2,1)S(1)} %fusion.82, f32[2,1024,128]{2,1,0:T(8,128)} %get-tuple-element.981, pred[]{:T(512)S(6)} %compare.11, bf16[512,2,128]{2,0,1:T(8,128)(2,1)S(1)} %copy.118), kind=kOutput, calls=%fused_computation.36.clone.1 | convolution fusion | flops 268959744 | bytes 4456449 | tf_op jit(solution)/shard_map/while/body/eval_jaxpr/gqs,gsd->gqd/dot_general | solution.py:144
  136.7 2.3 %copy.83 = bf16[2,512,512]{2,1,0:T(8,128)(2,1)} copy(bf16[2,512,512]{1,2,0:T(8,128)(2,1)} %get-tuple-element.405) | data formatting | bytes 2097152 | tf_op jit(solution)/shard_map/convert_element_type | solution.py:155
  139.1 1.3 convert_element_type.42
  140.8 60.1 %reduce-scatter.2.cloned.1.call-done = bf16[128,512]{1,0:T(8,128)(2,1)} async-done(((bf16[1024,512]{1,0:T(8,128)(2,1)}), bf16[128,512]{1,0:T(8,128)(2,1)}) %reduce-scatter.2.cloned.1.call-update) | async-done | bytes 131088 | tf_op jit(solution)/shard_map/reduce_scatter | solution.py:154
  201.0 0.9 maximum_bitcast_fusion.1
  201.9 1.3 collective-permute-start
  203.9 1.0 broadcast_in_dim_reshape.4
  205.0 13.8 %collective-permute-done = bf16[1,128,2560]{2,1,0:T(8,128)(2,1)S(1)} collective-permute-done((bf16[1,128,2560]{2,1,0:T(8,128)(2,1)S(1)}, bf16[1,128,2560]{2,1,0:T(8,128)(2,1)S(1)}, u32[]{:S(2)}, u32[]{:S(2)}) %collective-permute-start) | collective-permute-done | bytes 655392 | tf_op jit(solution)/shard_map/ppermute | solution.py:16
  218.8 0.8 slice.24
  219.6 0.7 fusion.30
  (91 shorter events, 9.2 us)
Async XLA Ops:
  7.2 3.6 %copy-start.5 = (bf16[1,128,256]{2,1,0:T(8,128)(2,1)S(1)}, bf16[1,128,256]{2,1,0:T(8,128)(2,1)}, u32[]{:S(2)}) copy-start(bf16[1,128,256]{2,1,0:T(8,128)(2,1)} %param.12) | copy-start | bytes 196612
  7.2 193.8 %reduce-scatter.2.cloned.1.call-start = ((), (), s32[]{:S(2)}) async-start(), calls=%async_computation.1 | async-start | bytes 1179648 | tf_op jit(solution)/shard_map/reduce_scatter | solution.py:154
  40.5 14.3 %copy-start.6 = (bf16[1,128,256]{2,1,0:T(8,128)(2,1)S(1)}, bf16[1,128,256]{2,1,0:T(8,128)(2,1)}, u32[]{:S(2)}) copy-start(bf16[1,128,256]{2,1,0:T(8,128)(2,1)} %param.13) | copy-start | bytes 196612
  83.7 13.0 %copy-start.4 = (bf16[1,128,2048]{2,1,0:T(8,128)(2,1)S(1)}, bf16[1,128,2048]{2,1,0:T(8,128)(2,1)}, u32[]{:S(2)}) copy-start(bf16[1,128,2048]{2,1,0:T(8,128)(2,1)} %param.14) | copy-start | bytes 1572868
  96.7 3.0 %copy-start.2 = (bf16[2,1024,128]{1,2,0:T(8,128)(2,1)}, bf16[2,1024,128]{1,2,0:T(8,128)(2,1)S(1)}, u32[]{:S(2)}) copy-start(bf16[2,1024,128]{1,2,0:T(8,128)(2,1)S(1)} %copy.79) | copy-start | bytes 1572868
  107.3 5.2 %copy-start = (f32[2,512,1024]{2,1,0:T(8,128)S(1)}, f32[2,512,1024]{2,1,0:T(8,128)}, u32[]{:S(2)}) copy-start(f32[2,512,1024]{2,1,0:T(8,128)} %fusion.81) | copy-start | bytes 12582916 | tf_op jit(solution)/shard_map/while
  107.3 5.2 %copy-start.1 = (pred[64,8,8,128]{3,1,2,0:T(8,128)(4,1)S(1)}, pred[64,8,8,128]{3,1,2,0:T(8,128)(4,1)}, u32[]{:S(2)}) copy-start(pred[64,8,8,128]{3,1,2,0:T(8,128)(4,1)} %copy.119) | copy-start | bytes 1572868 | tf_op jit(solution)/shard_map/while
  125.1 5.2 %copy-start = (f32[2,512,1024]{2,1,0:T(8,128)S(1)}, f32[2,512,1024]{2,1,0:T(8,128)}, u32[]{:S(2)}) copy-start(f32[2,512,1024]{2,1,0:T(8,128)} %fusion.81) | copy-start | bytes 12582916 | tf_op jit(solution)/shard_map/while
  125.1 5.2 %copy-start.1 = (pred[64,8,8,128]{3,1,2,0:T(8,128)(4,1)S(1)}, pred[64,8,8,128]{3,1,2,0:T(8,128)(4,1)}, u32[]{:S(2)}) copy-start(pred[64,8,8,128]{3,1,2,0:T(8,128)(4,1)} %copy.119) | copy-start | bytes 1572868 | tf_op jit(solution)/shard_map/while
  136.7 66.6 %copy-start.3 = (bf16[2,1024,128]{1,2,0:T(8,128)(2,1)S(1)}, bf16[2,1024,128]{1,2,0:T(8,128)(2,1)}, u32[]{:S(2)}) copy-start(bf16[2,1024,128]{1,2,0:T(8,128)(2,1)} %copy-done.2) | copy-start | bytes 1572868
  201.9 16.8 %collective-permute-start = (bf16[1,128,2560]{2,1,0:T(8,128)(2,1)S(1)}, bf16[1,128,2560]{2,1,0:T(8,128)(2,1)S(1)}, u32[]{:S(2)}, u32[]{:S(2)}) collective-permute-start(bf16[1,128,2560]{2,1,0:T(8,128)(2,1)S(1)} %maximum_bitcast_fusion.1), channel_id=1, source_target_pairs={{8,0},{9,1},{10,2},{11,3},{12,4},{13,5},{14,6},{15,7},{24,16},{25,... | collective-permute-start | bytes 1966088 | tf_op jit(solution)/shard_map/ppermute | solution.py:16
Sparse Core Ops, SparseCore 0:
  139.2 61.7 reduce-scatter.1
where the time goes:
time: 228 us; the launch traced here: 227 us
  waiting for transfers between devices  74 us (32%)
  blocking collectives  58.3 us (26%)
  matrix products  38 us (17%)
  local copies, waits for them, and re-layouts  25.5 us (11%)
  between operations  14.3 us (6%)
  other arithmetic  14 us (6%)
    reduce_scatter x1, waiting for transfers between devices, local(): lax.psum_scatter(block_terms.reshape(sequence, term_columns).astype(jnp.b...  60.1 us
    all_gather x1, blocking collectives, local(): lax.all_gather(section_key_state[0], 'ctx', axis=0, tiled=True)  29.5 us
    all_gather x1, blocking collectives, local(): lax.all_gather(section_value_state[0], 'ctx', axis=0, tiled=True)  28.8 us
    ppermute x1, waiting for transfers between devices, from_behind(): return lax.ppermute(x, axis, pairs)  13.8 us
    dot_general x4, matrix products, scores_of(): jnp.einsum('gqd,gsd->gqs', query_groups, key_block, preferred_element_typ...  11 us
    dot_general x2, matrix products, grads_of(): jnp.einsum('gqd,gsd->gqs', grad_groups, value_block, preferred_element_ty...  8.62 us
    dot_general x2, matrix products, out_step(): jnp.einsum('gqs,gsd->gqd', weights_low, value_block, preferred_element_ty...  6.99 us
    reduce_sum x2, other arithmetic, stat_step(): new_sum = new_sum + jnp.sum(jnp.exp(scores - new_max[..., None]), axis=-1)  6.32 us
  transfers between devices with their start and end apart: 2, of which 2 were waited for; matrix products, arithmetic and copies ran while one was open for 2% of the time, Pallas kernels for 0%

commit v1 on v0

--- a/solution.py
+++ b/solution.py
@@ -8,6 +8,28 @@
 KEY_VALUE_HEADS = 2
 HEAD_SIZE = 128
 BLK = 128
+
+
+def laid_out(tiles, dim):
+    shape = list(tiles.shape[1:])
+    shape[dim] *= tiles.shape[0]
+    return jnp.moveaxis(tiles, 0, dim).reshape(shape)
+
+
+def doubled(x, axis):
+    size = lax.axis_size(axis)
+    parts = x[None]
+    for level in range(size.bit_length() - 1):
+        bit = 1 << level
+        partner_block = lax.ppermute(parts, axis, [(i, i ^ bit) for i in range(size)])
+        both = jnp.stack([parts, partner_block])
+        upper = lax.axis_index(axis) >> level & 1
+        parts = jnp.where(upper == 0, both, both[::-1]).reshape(-1, *x.shape)
+    return parts
+
+
+def doubled_up(array, axis, dim):
+    return laid_out(doubled(array, axis), dim)
 
 
 def from_behind(x, axis, by):
@@ -64,7 +86,7 @@
     grad_groups = to_groups(out_grad[0], shard_rows, group_width)
     key_all, value_all = (
         lax.all_gather(section_key_state[0], "ctx", axis=0, tiled=True),
-        lax.all_gather(section_value_state[0], "ctx", axis=0, tiled=True),
+        doubled_up(section_value_state[0], "ctx", 0),
     )
 
     def block_inputs(first_row, total_size):

time: 228 us -> 212 us (0.930)
  blocking collectives: 58.3 us -> 27.9 us
  starting transfers between devices: 1.33 us -> 5.98 us
  waiting for transfers between devices: 74 us -> 77.6 us
  other arithmetic: 14 us -> 16.8 us
  local copies, waits for them, and re-layouts: 25.5 us -> 28.3 us
    all_gather x1 -> x0, blocking collectives: 28.8 us -> none  [local(): lax.all_gather(section_value_state[0], 'ctx', axis=0, tiled=True)]
    ppermute x0 -> x3, starting transfers between devices: none -> 4.65 us  [doubled(): lax.ppermute(parts, axis, [(i, i ^ bit) for i in range(size)])]
    ppermute x0 -> x3, waiting for transfers between devices: none -> 2.93 us  [doubled(): lax.ppermute(parts, axis, [(i, i ^ bit) for i in range(size)])]
  transfers between devices with their start and end apart: 2 -> 5, of which waited for: 2 -> 3; matrix products, arithmetic and copies ran while one was open for 2% -> 11% of each run, Pallas kernels for 0% -> 0%
where the time goes in v1:
time: 212 us; the launch traced here: 211 us
  waiting for transfers between devices  77.6 us (37%)
  matrix products  37.9 us (18%)
  local copies, waits for them, and re-layouts  28.3 us (13%)
  blocking collectives  27.9 us (13%)
  other arithmetic  16.8 us (8%)
  between operations  14.3 us (7%)
  starting transfers between devices  5.98 us (3%)
    reduce_scatter x1, waiting for transfers between devices, local(): lax.psum_scatter(block_terms.reshape(sequence, term_columns).astype(jnp.b...  60.9 us
    all_gather x1, blocking collectives, local(): lax.all_gather(section_key_state[0], 'ctx', axis=0, tiled=True)  27.9 us
    ppermute x1, waiting for transfers between devices, from_behind(): return lax.ppermute(x, axis, pairs)  13.8 us
    dot_general x4, matrix products, scores_of(): jnp.einsum('gqd,gsd->gqs', query_groups, key_block, preferred_element_typ...  11 us
    dot_general x2, matrix products, grads_of(): jnp.einsum('gqd,gsd->gqs', grad_groups, value_block, preferred_element_ty...  8.63 us
    dot_general x2, matrix products, out_step(): jnp.einsum('gqs,gsd->gqd', weights_low, value_block, preferred_element_ty...  6.91 us
    reduce_sum x2, other arithmetic, stat_step(): new_sum = new_sum + jnp.sum(jnp.exp(scores - new_max[..., None]), axis=-1)  6.32 us
    dot_general x2, matrix products, back_step(): jnp.einsum('gqs,gsd->gqd', score_grad, key_block, preferred_element_type=...  5.03 us
  transfers between devices with their start and end apart: 5, of which 3 were waited for; matrix products, arithmetic and copies ran while one was open for 11% of the time, Pallas kernels for 0%

profile of v1, /device:TPU:0, one launch (start us, length us, event | category | flops | bytes accessed | tf_op | source)
XLA Modules:
  0.0 210.7 jit_solution(2678711700474840828)
XLA Ops:
  7.2 3.0 %collective-permute-start = (bf16[1,128,256]{2,1,0:T(8,128)(2,1)}, bf16[1,128,256]{2,1,0:T(8,128)(2,1)S(1)}, u32[]{:S(2)}, u32[]{:S(2)}) collective-permute-start(bf16[1,128,256]{2,1,0:T(8,128)(2,1)} %param.13), channel_id=1, source_target_pairs={{0,1},{1,0},{2,3},{3,2},{4,5},{5,4},{6,7},{7,6},{8,9},{9,8},{10,11... | collective-permute-start | bytes 196616 | tf_op jit(solution)/shard_map/ppermute | solution.py:24
  11.1 0.9 copy.76
  12.0 27.9 %all-gather = bf16[1,1024,256]{1,2,0:T(8,128)(2,1)S(1)} all-gather(bf16[1,128,256]{1,2,0:T(8,128)(2,1)S(1)} %copy.76), channel_id=2, replica_groups=mesh['dp'=2,'pipe'=2,'ctx'=8] {'ctx'}, dimensions={1}, use_global_device_ids=true | all-gather | bytes 589824 | tf_op jit(solution)/shard_map/all_gather | solution.py:88
  40.2 0.9 pad_maximum_fusion.2
  41.9 1.1 copy.96
  44.3 2.9 %collective-permute-done.1 = bf16[2,128,256]{2,1,0:T(8,128)(2,1)S(1)} collective-permute-done((bf16[2,128,256]{2,1,0:T(8,128)(2,1)S(1)}, bf16[2,128,256]{2,1,0:T(8,128)(2,1)S(1)}, u32[]{:S(2)}, u32[]{:S(2)}) %collective-permute-start.1) | collective-permute-done | bytes 131104 | tf_op jit(solution)/shard_map/ppermute | solution.py:24
  47.3 0.9 copy.79
  48.2 0.9 collective-permute-start.2
  49.0 14.3 %while.43 = (s32[]{:T(128)}, f32[2,1024]{1,0:T(2,128)S(1)}, f32[2,1024]{1,0:T(2,128)S(1)}, s32[128]{0:T(128)S(1)}, s32[1024]{0:T(1024)S(1)}, /*index=5*/s32[1024...) while((s32[]{:T(128)}, f32[2,1024]{1,0:T(2,128)S(1)}, ...), condition=%wide.region_6.7_spmd.clone, body=%wide.region_3.6_spmd.clone.sunk | while | flops 275982336 | bytes 13096130 | solution.py:128
  50.1 2.9 %fusion.66 = (f32[2,1024]{1,0:T(2,128)S(1)}, f32[2,512,1024]{2,1,0:T(8,128)}) fusion(pred[1024,512]{0,1:T(8,128)(4,1)S(1)} %bitcast.222, bf16[2,1024,128]{2,1,0:T(8,128)(2,1)S(1)} %get-tuple-element.917, bf16[512,2,128]{2,0,1:T(8,128)(2,1)S(1)} %copy.117), kind=kOutput, calls=%fused_computation.2.clone.1 | convolution fusion | flops 271579136 | bytes 5513216 | tf_op jit(solution)/shard_map/while/body/eval_jaxpr/gqd,gsd->gqs/dot_general | solution.py:112
  53.0 3.2 %exponential_reduce_fusion.2 = f32[2,1024]{1,0:T(2,128)S(1)} fusion(f32[2,512,1024]{2,1,0:T(8,128)} %get-tuple-element.854, f32[2,1024]{1,0:T(2,128)S(1)} %fusion.67, pred[1024,512]{0,1:T(8,128)(4,1)S(1)} %bitcast.223), kind=kLoop, calls=%fused_computation.1.clone.1 | loop fusion | flops 4192256 | bytes 4734976 | tf_op jit(solution)/shard_map/while/body/eval_jaxpr/reduce_sum | solution.py:123
  57.3 2.9 %fusion.66 = (f32[2,1024]{1,0:T(2,128)S(1)}, f32[2,512,1024]{2,1,0:T(8,128)}) fusion(pred[1024,512]{0,1:T(8,128)(4,1)S(1)} %bitcast.222, bf16[2,1024,128]{2,1,0:T(8,128)(2,1)S(1)} %get-tuple-element.917, bf16[512,2,128]{2,0,1:T(8,128)(2,1)S(1)} %copy.117), kind=kOutput, calls=%fused_computation.2.clone.1 | convolution fusion | flops 271579136 | bytes 5513216 | tf_op jit(solution)/shard_map/while/body/eval_jaxpr/gqd,gsd->gqs/dot_general | solution.py:112
  60.1 3.2 %exponential_reduce_fusion.2 = f32[2,1024]{1,0:T(2,128)S(1)} fusion(f32[2,512,1024]{2,1,0:T(8,128)} %get-tuple-element.854, f32[2,1024]{1,0:T(2,128)S(1)} %fusion.67, pred[1024,512]{0,1:T(8,128)(4,1)S(1)} %bitcast.223), kind=kLoop, calls=%fused_computation.1.clone.1 | loop fusion | flops 4192256 | bytes 4734976 | tf_op jit(solution)/shard_map/while/body/eval_jaxpr/reduce_sum | solution.py:123
  64.1 1.0 reshape.304
  65.4 1.3 pad_maximum_fusion
  67.0 1.2 reshape_reshape.3
  68.1 11.4 %while.44 = (s32[]{:T(128)}, f32[2,1024,128]{2,1,0:T(8,128)}, s32[128]{0:T(128)S(1)}, s32[1024]{0:T(1024)S(1)}, s32[1024]{0:T(1024)S(1)}, /*index=5*/s32[128]{0:...) while((s32[]{:T(128)}, f32[2,1024,128]{2,1,0:T(8,128)}, ...), condition=%wide.region_8.9_spmd.clone, body=%wide.region_7.8_spmd.clone.sunk | while | flops 541786112 | bytes 7492809 | solution.py:141
  69.0 1.0 constant_dynamic-slice_fusion.9
  70.4 2.8 %fusion.72 = f32[2,1024,128]{2,1,0:T(8,128)} fusion(bf16[2,1024,128]{2,1,0:T(8,128)(2,1)S(1)} %get-tuple-element.957, f32[2,1024]{1,0:T(2,128)S(1)} %get-tuple-element.958, pred[1024,512]{0,1:T(8,128)(4,1)S(1)} %bitcast.236, f32[2,1024,128]{2,1,0:T(8,128)} %get-tuple-element.937, pred[]{:T(512)S(6)} %compare.10, ...), kind=kOutput, calls=%fused_computation.18.clone.1 | convolution fusion | flops 541589504 | bytes 3678209 | tf_op jit(solution)/shard_map/while/body/eval_jaxpr/gqs,gsd->gqd/dot_general | solution.py:136
  74.1 1.0 constant_dynamic-slice_fusion.9
  75.4 4.1 %fusion.72 = f32[2,1024,128]{2,1,0:T(8,128)} fusion(bf16[2,1024,128]{2,1,0:T(8,128)(2,1)S(1)} %get-tuple-element.957, f32[2,1024]{1,0:T(2,128)S(1)} %get-tuple-element.958, pred[1024,512]{0,1:T(8,128)(4,1)S(1)} %bitcast.236, f32[2,1024,128]{2,1,0:T(8,128)} %get-tuple-element.937, pred[]{:T(512)S(6)} %compare.10, ...), kind=kOutput, calls=%fused_computation.18.clone.1 | convolution fusion | flops 541589504 | bytes 3678209 | tf_op jit(solution)/shard_map/while/body/eval_jaxpr/gqs,gsd->gqd/dot_general | solution.py:136
  79.5 1.4 copy.82
  81.0 1.4 multiply_reduce_fusion
  82.4 37.1 %while.45 = (s32[]{:T(128)}, f32[2,1024,128]{2,1,0:T(8,128)}, bf16[2,512,512]{1,2,0:T(8,128)(2,1)}, s32[128]{0:T(128)S(1)}, s32[2]{0:T(128)S(1)}, /*index=5*/s32...) while((s32[]{:T(128)}, f32[2,1024,128]{2,1,0:T(8,128)}, ...), condition=%wide.region_11.12_spmd.clone, body=%wide.region_10.11_spmd.clone.sunk | while | flops 1355481088 | bytes 49190700 | solution.py:172
  84.4 1.1 copy.122
  85.5 1.0 constant_dynamic-slice_fusion.10
  86.7 2.6 %fusion.83 = f32[2,512,1024]{2,1,0:T(8,128)} fusion(bf16[2,1024,128]{1,2,0:T(8,128)(2,1)S(1)} %get-tuple-element.1009, bf16[512,2,128]{2,0,1:T(8,128)(2,1)S(1)} %copy.121), kind=kOutput, calls=%fused_computation.41.clone.1 | convolution fusion | flops 268435456 | bytes 4980736 | tf_op jit(solution)/shard_map/while/body/eval_jaxpr/gqd,gsd->gqs/dot_general | solution.py:112
  90.2 4.3 %fusion.84 = bf16[2,1024,512]{1,2,0:T(8,128)(2,1)S(1)} fusion(f32[2,512,1024]{2,1,0:T(8,128)} %fusion.83, bf16[2,1024,128]{1,2,0:T(8,128)(2,1)} %get-tuple-element.1012, f32[2,1024]{1,0:T(2,128)S(1)} %get-tuple-element.1013, f32[2,1024]{1,0:T(2,128)S(1)} %get-tuple-element.1010, pred[1024,512]{0,1:T(8,128)(4,1)} %bitcast.234, ...), kind=kOutput, calls=%fused_computation.28.clone.1 | convolution fusion | flops 275775488 | bytes 7618560 | tf_op jit(solution)/shard_map/while/body/eval_jaxpr/gqd,gsd->gqs/dot_general | solution.py:146
  94.5 0.8 fusion.86
  95.3 2.3 %fusion.85 = bf16[2,512,128]{1,2,0:T(8,128)(2,1)S(1)} fusion(bf16[2,1024,128]{1,2,0:T(8,128)(2,1)} %get-tuple-element.1012, f32[2,512,1024]{2,1,0:T(8,128)S(1)} %copy-done, f32[2,1024]{1,0:T(2,128)S(1)} %get-tuple-element.1010, pred[1024,512]{0,1:T(8,128)(4,1)S(1)} %bitcast.235), kind=kOutput, calls=%fused_computation.33.clone.1 | convolution fusion | flops 272629760 | bytes 5513216 | tf_op jit(solution)/shard_map/while/body/eval_jaxpr/gqs,gqd->sgd/dot_general | solution.py:158
  97.7 0.8 fusion.87
  98.5 1.9 convolution_add_fusion.2
  102.3 1.1 copy.122
  103.4 1.0 constant_dynamic-slice_fusion.10
  104.5 2.6 %fusion.83 = f32[2,512,1024]{2,1,0:T(8,128)} fusion(bf16[2,1024,128]{1,2,0:T(8,128)(2,1)S(1)} %get-tuple-element.1009, bf16[512,2,128]{2,0,1:T(8,128)(2,1)S(1)} %copy.121), kind=kOutput, calls=%fused_computation.41.clone.1 | convolution fusion | flops 268435456 | bytes 4980736 | tf_op jit(solution)/shard_map/while/body/eval_jaxpr/gqd,gsd->gqs/dot_general | solution.py:112
  108.0 4.3 %fusion.84 = bf16[2,1024,512]{1,2,0:T(8,128)(2,1)S(1)} fusion(f32[2,512,1024]{2,1,0:T(8,128)} %fusion.83, bf16[2,1024,128]{1,2,0:T(8,128)(2,1)} %get-tuple-element.1012, f32[2,1024]{1,0:T(2,128)S(1)} %get-tuple-element.1013, f32[2,1024]{1,0:T(2,128)S(1)} %get-tuple-element.1010, pred[1024,512]{0,1:T(8,128)(4,1)} %bitcast.234, ...), kind=kOutput, calls=%fused_computation.28.clone.1 | convolution fusion | flops 275775488 | bytes 7618560 | tf_op jit(solution)/shard_map/while/body/eval_jaxpr/gqd,gsd->gqs/dot_general | solution.py:146
  112.3 0.8 fusion.86
  113.2 2.3 %fusion.85 = bf16[2,512,128]{1,2,0:T(8,128)(2,1)S(1)} fusion(bf16[2,1024,128]{1,2,0:T(8,128)(2,1)} %get-tuple-element.1012, f32[2,512,1024]{2,1,0:T(8,128)S(1)} %copy-done, f32[2,1024]{1,0:T(2,128)S(1)} %get-tuple-element.1010, pred[1024,512]{0,1:T(8,128)(4,1)S(1)} %bitcast.235), kind=kOutput, calls=%fused_computation.33.clone.1 | convolution fusion | flops 272629760 | bytes 5513216 | tf_op jit(solution)/shard_map/while/body/eval_jaxpr/gqs,gqd->sgd/dot_general | solution.py:158
  115.5 0.8 fusion.87
  116.4 3.1 %convolution_add_fusion.2 = f32[2,1024,128]{2,1,0:T(8,128)} fusion(bf16[2,1024,512]{1,2,0:T(8,128)(2,1)S(1)} %fusion.84, f32[2,1024,128]{2,1,0:T(8,128)} %get-tuple-element.983, pred[]{:T(512)S(6)} %compare.11, bf16[512,2,128]{2,0,1:T(8,128)(2,1)S(1)} %copy.121), kind=kOutput, calls=%fused_computation.36.clone.1 | convolution fusion | flops 268959744 | bytes 4456449 | tf_op jit(solution)/shard_map/while/body/eval_jaxpr/gqs,gsd->gqd/dot_general | solution.py:166
  119.5 2.3 %copy.86 = bf16[2,512,512]{2,1,0:T(8,128)(2,1)} copy(bf16[2,512,512]{1,2,0:T(8,128)(2,1)} %get-tuple-element.405) | data formatting | bytes 2097152 | tf_op jit(solution)/shard_map/convert_element_type | solution.py:177
  121.9 1.3 convert_element_type.42
  123.7 60.9 %reduce-scatter.2.cloned.1.call-done = bf16[128,512]{1,0:T(8,128)(2,1)} async-done(((bf16[1024,512]{1,0:T(8,128)(2,1)}), bf16[128,512]{1,0:T(8,128)(2,1)}) %reduce-scatter.2.cloned.1.call-update) | async-done | bytes 131088 | tf_op jit(solution)/shard_map/reduce_scatter | solution.py:176
  184.5 0.9 maximum_bitcast_fusion.1
  185.5 1.3 collective-permute-start.3
  187.5 1.0 broadcast_in_dim_reshape.4
  188.5 13.8 %collective-permute-done.3 = bf16[1,128,2560]{2,1,0:T(8,128)(2,1)S(1)} collective-permute-done((bf16[1,128,2560]{2,1,0:T(8,128)(2,1)S(1)}, bf16[1,128,2560]{2,1,0:T(8,128)(2,1)S(1)}, u32[]{:S(2)}, u32[]{:S(2)}) %collective-permute-start.3) | collective-permute-done | bytes 655392 | tf_op jit(solution)/shard_map/ppermute | solution.py:38
  202.3 0.8 slice.24
  (100 shorter events, 15.2 us)
Async XLA Ops:
  7.2 177.4 %reduce-scatter.2.cloned.1.call-start = ((), (), s32[]{:S(2)}) async-start(), calls=%async_computation.1 | async-start | bytes 1179648 | tf_op jit(solution)/shard_map/reduce_scatter | solution.py:176
  7.2 33.0 %collective-permute-start = (bf16[1,128,256]{2,1,0:T(8,128)(2,1)}, bf16[1,128,256]{2,1,0:T(8,128)(2,1)S(1)}, u32[]{:S(2)}, u32[]{:S(2)}) collective-permute-start(bf16[1,128,256]{2,1,0:T(8,128)(2,1)} %param.13), channel_id=1, source_target_pairs={{0,1},{1,0},{2,3},{3,2},{4,5},{5,4},{6,7},{7,6},{8,9},{9,8},{10,11... | collective-permute-start | bytes 196616 | tf_op jit(solution)/shard_map/ppermute | solution.py:24
  41.1 6.1 %collective-permute-start.1 = (bf16[2,128,256]{2,1,0:T(8,128)(2,1)S(1)}, bf16[2,128,256]{2,1,0:T(8,128)(2,1)S(1)}, u32[]{:S(2)}, u32[]{:S(2)}) collective-permute-start(bf16[2,128,256]{2,1,0:T(8,128)(2,1)S(1)} %get-tuple-element.665), channel_id=1, source_target_pairs={{0,2},{1,3},{2,0},{3,1},{4,6},{5,7},{6,4},{7,5},{8,10},{9,11},{10,... | collective-permute-start | bytes 393224 | tf_op jit(solution)/shard_map/ppermute | solution.py:24
  48.2 17.2 %collective-permute-start.2 = (bf16[4,128,256]{1,0,2:T(4,128)(2,1)}, bf16[4,128,256]{1,0,2:T(4,128)(2,1)}, u32[]{:S(2)}, u32[]{:S(2)}) collective-permute-start(bf16[4,128,256]{1,0,2:T(4,128)(2,1)} %copy.79), channel_id=1, source_target_pairs={{0,4},{1,5},{2,6},{3,7},{4,0},{5,1},{6,2},{7,3},{8,12},{9,13},{10,... | collective-permute-start | bytes 786440 | tf_op jit(solution)/shard_map/ppermute | solution.py:24
  49.0 14.4 %copy-start.4 = (bf16[1,128,2048]{2,1,0:T(8,128)(2,1)S(1)}, bf16[1,128,2048]{2,1,0:T(8,128)(2,1)}, u32[]{:S(2)}) copy-start(bf16[1,128,2048]{2,1,0:T(8,128)(2,1)} %param.14) | copy-start | bytes 1572868
  80.9 1.4 copy-start.2
  90.1 5.2 %copy-start = (f32[2,512,1024]{2,1,0:T(8,128)S(1)}, f32[2,512,1024]{2,1,0:T(8,128)}, u32[]{:S(2)}) copy-start(f32[2,512,1024]{2,1,0:T(8,128)} %fusion.83) | copy-start | bytes 12582916 | tf_op jit(solution)/shard_map/while
  90.2 5.2 %copy-start.1 = (pred[64,8,8,128]{3,1,2,0:T(8,128)(4,1)S(1)}, pred[64,8,8,128]{3,1,2,0:T(8,128)(4,1)}, u32[]{:S(2)}) copy-start(pred[64,8,8,128]{3,1,2,0:T(8,128)(4,1)} %copy.122) | copy-start | bytes 1572868 | tf_op jit(solution)/shard_map/while
  108.0 5.2 %copy-start = (f32[2,512,1024]{2,1,0:T(8,128)S(1)}, f32[2,512,1024]{2,1,0:T(8,128)}, u32[]{:S(2)}) copy-start(f32[2,512,1024]{2,1,0:T(8,128)} %fusion.83) | copy-start | bytes 12582916 | tf_op jit(solution)/shard_map/while
  108.0 5.2 %copy-start.1 = (pred[64,8,8,128]{3,1,2,0:T(8,128)(4,1)S(1)}, pred[64,8,8,128]{3,1,2,0:T(8,128)(4,1)}, u32[]{:S(2)}) copy-start(pred[64,8,8,128]{3,1,2,0:T(8,128)(4,1)} %copy.122) | copy-start | bytes 1572868 | tf_op jit(solution)/shard_map/while
  119.5 67.3 %copy-start.3 = (bf16[2,1024,128]{1,2,0:T(8,128)(2,1)S(1)}, bf16[2,1024,128]{1,2,0:T(8,128)(2,1)}, u32[]{:S(2)}) copy-start(bf16[2,1024,128]{1,2,0:T(8,128)(2,1)} %copy-done.2) | copy-start | bytes 1572868
  185.5 16.8 %collective-permute-start.3 = (bf16[1,128,2560]{2,1,0:T(8,128)(2,1)S(1)}, bf16[1,128,2560]{2,1,0:T(8,128)(2,1)S(1)}, u32[]{:S(2)}, u32[]{:S(2)}) collective-permute-start(bf16[1,128,2560]{2,1,0:T(8,128)(2,1)S(1)} %maximum_bitcast_fusion.1), channel_id=1, source_target_pairs={{8,0},{9,1},{10,2},{11,3},{12,4},{13,5},{14,6},{15,7},{24,16},{25,... | collective-permute-start | bytes 1966088 | tf_op jit(solution)/shard_map/ppermute | solution.py:38
Sparse Core Ops, SparseCore 0:
  122.0 62.5 reduce-scatter.1
